TPU v7x, 32 devices: a whole 2x2x4 slice. The times are simulated.
32 devices in a mesh: seq: 2 (over y), rep: 4 (over z), tensor: 4 (over x, core).
Axes of the slice: x: 2, y: 2, z: 4, core: 2. Of those that a mesh axis runs over, the one named last changes fastest.
Arguments:
- key_value_rows: bfloat16 [4, 3072, 8, 256], P('rep', ('seq', 'tensor')), may hold values from -32 to 32
- queries: bfloat16 [4, 64, 64, 128], P('rep', None, 'tensor'), may hold values from -136 to 136
- w_comp: bfloat16 [2048, 512], replicated, may hold values from -0.125 to 0.125
- latent_gain: bfloat16 [512], replicated, may hold values from 0.099609375 to 1.8984375
- w_up: bfloat16 [8, 512, 256], P('tensor'), may hold values from -0.25 to 0.25
- w_out: bfloat16 [8192, 8192], P('tensor', 'seq'), may hold values from -0.0625 to 0.0625
- replica_order: int32 [4], replicated, may hold values from 0 to 3, each once
Outputs:
- decoded: bfloat16 [4, 64, 8192], P('rep', None, 'seq')
Inputs may be any that keep to these rules, and one draw needn't show every extreme that they name: replica_order is a permutation of the prompts.
All inputs are finite; a program needn't handle non-finite values.
Results may differ from a plain program's by a relative error of at most 0.01.
Values may be sent and summed in bfloat16 or wider, within the bound.
No kernel may reach another device: no remote copies, remote signals or barrier semaphores. Data moves between devices by JAX's collectives and lax.ppermute only.
A program may use at most 64 MiB of HBM per device.

v0:
```python
import itertools
import math

import jax
import jax.numpy as jnp
from jax import lax
from jax.experimental import pallas as pl
from jax.experimental.pallas import tpu as pltpu
from jax.sharding import PartitionSpec as P

BF16, F32 = jnp.bfloat16, jnp.float32
MIB = 1024 * 1024
IN_VMEM = pl.BlockSpec(memory_space=pltpu.VMEM)
IN_SMEM = pl.BlockSpec(memory_space=pltpu.SMEM)
IN_HBM = pl.BlockSpec(memory_space=pltpu.HBM)
COPIES = 8
PARTS = 2


def shape(dims, dtype):
    return jax.ShapeDtypeStruct(dims, dtype)


def call(body, name, outs, operands, vmem, scratch=(), smem_in=0, smem_out=0, hbm_in=0, cost=None):
    kept = len(operands) - hbm_in
    specs = [IN_SMEM] * smem_in + [IN_VMEM] * (kept - smem_in) + [IN_HBM] * hbm_in
    operands = [
        *operands[:kept],
        *(pltpu.with_memory_space_constraint(operand, pltpu.HBM) for operand in operands[kept:]),
    ]
    out_specs = [IN_VMEM] * (len(outs) - smem_out) + [IN_SMEM] * smem_out
    return pl.pallas_call(
        body,
        out_shape=outs,
        in_specs=specs,
        out_specs=out_specs,
        scratch_shapes=list(scratch),
        compiler_params=pltpu.CompilerParams(vmem_limit_bytes=vmem * MIB),
        cost_estimate=cost,
        name=name,
    )(*operands)


def cost(flops, moved, exps=0):
    return pl.CostEstimate(flops=int(flops), bytes_accessed=int(moved), transcendentals=int(exps))


def dot(a, b):
    return jnp.dot(a, b, preferred_element_type=F32)


def compress(rows, weight, gain):
    projected = dot(rows, weight)
    scale = lax.rsqrt(jnp.mean(projected * projected, axis=-1, keepdims=True) + 1e-06)
    return (projected * scale * gain.astype(F32)[None]).astype(BF16)


def order_index(replica_order, orders):
    table = jnp.array(orders, jnp.int32)
    match = jnp.all(table == replica_order[None], axis=1)
    return jnp.sum(jnp.where(match, lax.iota(jnp.int32, len(orders)), 0))


def route_pairs(order, back):
    return [(p, r) if back else (r, p) for r, p in enumerate(order)]


def route(value, index, orders, back):
    def branch(order):
        return lambda v: lax.ppermute(v, "rep", route_pairs(order, back))

    return lax.switch(index, [branch(o) for o in orders], value)


def shift(value, axis, hops):
    size = lax.axis_size(axis)
    return lax.ppermute(value, axis, [(i, (i + hops) % size) for i in range(size)])


def swap(value, axis, bit):
    pairs = [(i, i ^ bit) for i in range(lax.axis_size(axis))]
    return lax.ppermute(value, axis, pairs)


def cross(value, seq_core):
    pairs = [(i, i ^ (4 if i % 2 == seq_core else 2)) for i in range(8)]
    return lax.ppermute(value, ("seq", "tensor"), pairs)


def compress_kernel(chunks, *refs):
    (order_hbm, rows_hbm, weight_hbm, gain_hbm, query_hbm, latent_ref, half_ref, index_ref, pick_ref) = refs[:9]
    (order_ref, rows_ref, weight_ref, gain_ref, query_ref, wide, packed, sems) = refs[9:]
    tokens, groups, width = rows_ref.shape
    chunk = tokens // chunks
    copies = [pltpu.make_async_copy(order_hbm, order_ref, sems.at[0])]
    for i in range(chunks):
        at = pl.ds(i * chunk, chunk)
        copies.append(pltpu.make_async_copy(rows_hbm.at[0, at], rows_ref.at[at], sems.at[1 + i]))
    for group in range(groups):
        at = pl.ds(group * width, width)
        copies.append(
            pltpu.make_async_copy(weight_hbm.at[at], weight_ref.at[at], sems.at[1 + chunks + group])
        )
    copies.append(pltpu.make_async_copy(gain_hbm, gain_ref, sems.at[1 + chunks + groups]))
    copies.append(pltpu.make_async_copy(query_hbm.at[0], query_ref, sems.at[2 + chunks + groups]))
    for copy in copies:
        copy.start()

    copies[0].wait()
    count = order_ref.shape[0]
    here = lax.axis_index("rep")
    index, wanted, wanted_beside = 0, 0, 0
    for i in range(count):
        wanted = jnp.where(order_ref[i] == here, i, wanted)
        wanted_beside = jnp.where(order_ref[i] == (here ^ 1), i, wanted_beside)
        smaller = 0
        for j in range(i + 1, count):
            smaller = smaller + (order_ref[j] < order_ref[i]).astype(jnp.int32)
        index = index + smaller * math.factorial(count - 1 - i)
    index_ref[0] = index
    pick_ref[0] = (wanted_beside == (here ^ 2)).astype(jnp.int32)
    pick_ref[1] = jnp.where(wanted == here, 0, jnp.where(wanted == (here ^ 2), 1, 2))

    lanes = wide.shape[2]
    for i in range(chunks):
        copies[1 + i].wait()
        at = slice(i * chunk * groups, (i + 1) * chunk * groups)
        for part in range(wide.shape[0]):
            values = rows_ref[i * chunk : (i + 1) * chunk, :, part * lanes : (part + 1) * lanes]
            wide[part, at] = values.astype(F32).reshape(chunk * groups, lanes)
        for group in range(groups):
            for part in range(wide.shape[0]):
                start = group * width + part * lanes
                picked = wide[part, pl.ds(at.start + group, chunk, stride=groups), :]
                packed[i * chunk : (i + 1) * chunk, start : start + lanes] = picked.astype(BF16)
    for group in range(groups):
        copies[1 + chunks + group].wait()
    copies[1 + chunks + groups].wait()
    gain = gain_ref[...].astype(F32)[None]
    projected = dot(packed[...], weight_ref[...])
    scale = lax.rsqrt(jnp.mean(projected * projected, axis=-1, keepdims=True) + 1e-06)
    latent_ref[...] = (projected * scale * gain).astype(BF16)

    copies[2 + chunks + groups].wait()
    new_count, heads, head_size = query_ref.shape
    query = query_ref[...].astype(F32)
    upper = lax.axis_index("seq") == 1
    query = jnp.where(upper, query[:, heads // 2 :], query[:, : heads // 2])
    half_ref[...] = query.reshape(half_ref.shape).astype(BF16)


def score_kernel(parts, *refs):
    latent_refs, (lift_ref, query_ref), (score_ref, value_ref, top_ref) = (
        refs[:parts],
        refs[parts : parts + 2],
        refs[parts + 2 :],
    )
    head_size = query_ref.shape[-1]
    lift = lift_ref[lax.axis_index("seq")]
    query = query_ref[...]
    top = None
    for part, latent_ref in enumerate(latent_refs):
        tokens = latent_ref.shape[0]
        at = slice(part * tokens, (part + 1) * tokens)
        lifted = dot(latent_ref[...], lift).astype(BF16)
        score = lax.dot_general(
            lifted[:, :head_size], query, (((1,), (1,)), ((), ())), preferred_element_type=F32
        )
        score_ref[at] = score
        value_ref[at] = lifted[:, head_size:]
        part_top = jnp.max(score, axis=0, keepdims=True)
        top = part_top if top is None else jnp.maximum(top, part_top)
    top_ref[...] = jnp.broadcast_to(top, top_ref.shape)


def fetch_kernel(own, weight_ref, *refs):
    *held_refs, sems = refs
    depth, columns = held_refs[0].shape
    rows = depth // COPIES
    group = lax.axis_index("seq") if own else 1 - lax.axis_index("seq")
    core = lax.axis_index("tensor") % 2
    copies = []
    for part, held_ref in enumerate(held_refs):
        first = 0 if own else pl.multiple_of((core if part else 1 - core) * columns, columns)
        for i in range(COPIES):
            start = pl.multiple_of(group * depth + i * rows, rows)
            source = weight_ref.at[pl.ds(start, rows), pl.ds(first, columns)]
            target = held_ref.at[pl.ds(i * rows, rows)]
            copies.append(pltpu.make_async_copy(source, target, sems.at[part, i]))
    for copy in copies:
        copy.start()
    for copy in copies:
        copy.wait()


def fetch(name, own, weight):
    depth, columns = weight.shape[0] // 2, weight.shape[1]
    blocks = [(depth, columns)] if own else [(depth, columns // 2)] * 2
    return call(
        lambda *refs: fetch_kernel(own, *refs),
        name,
        [pltpu.VMEM(block, weight.dtype) for block in blocks],
        [weight],
        4,
        scratch=[pltpu.SemaphoreType.DMA((len(blocks), COPIES))],
        hbm_in=1,
        cost=cost(0, 0),
    )


def choose(pick, refs, out_ref):
    for i, ref in enumerate(refs):

        @pl.when(pick == i)
        def _():
            out_ref[...] = ref[...]


def pass_kernel(pick_ref, own_ref, second_ref, out_ref):
    choose(pick_ref[0], (own_ref, second_ref), out_ref)


def choose_and_score_kernel(parts, pick_ref, *refs):
    *refs, score_ref, value_ref, top_ref, query_ref = refs
    choose(pick_ref[1], refs[parts + 1 :], query_ref)
    score_kernel(parts, *refs[: parts + 1], query_ref, score_ref, value_ref, top_ref)


def score_call(name, latents, lift, query, pick=None):
    queries = [query] if pick is None else query
    tokens = sum(latent.shape[0] for latent in latents)
    rows, head_size = queries[0].shape
    outs = [shape((tokens, rows), F32), shape((tokens, head_size), BF16), shape((8, rows), F32)]
    operands = [*latents, lift, *queries]
    estimate = cost(0, 0)
    if pick is None:
        body = lambda *refs: score_kernel(len(latents), *refs)
        return call(body, name, outs, operands, 16, cost=estimate)
    body = lambda *refs: choose_and_score_kernel(len(latents), *refs)
    outs.append(shape((rows, head_size), BF16))
    return call(body, name, outs, [pick, *operands], 16, smem_in=1, cost=estimate)


def attend_kernel(part, block, *refs):
    (*score_refs, out_ref, turned) = refs
    new_count = out_ref.shape[0]
    rows = slice(part * turned.shape[0], (part + 1) * turned.shape[0])
    triples = [score_refs[i : i + 3] for i in range(0, len(score_refs), 3)]
    head_size = triples[0][1].shape[-1]
    coef = head_size ** (-0.5) * math.log2(math.e)
    top = triples[0][2][:1, rows]
    for triple in triples[1:]:
        top = jnp.maximum(top, triple[2][:1, rows])
    total = jnp.zeros_like(top)
    summed = jnp.zeros((head_size, top.shape[1]), F32)
    for score_ref, value_ref, _ in triples:
        for start in range(0, score_ref.shape[0], block):
            at = slice(start, start + block)
            expo = jnp.exp2((score_ref[at, rows] - top) * coef)
            total += jnp.sum(expo, axis=0, keepdims=True)
            summed += lax.dot_general(
                value_ref[at], expo.astype(BF16), (((0,), (0,)), ((), ())), preferred_element_type=F32
            )
    turned[...] = (summed / total).T
    heads = turned.shape[0] // new_count
    for head in range(heads):
        out_ref[:, head * head_size : (head + 1) * head_size] = turned[
            pl.ds(head, new_count, stride=heads), :
        ].astype(BF16)


def project_kernel(tile, *refs):
    *row_refs, weight_ref, out_ref = refs
    rows = jnp.concatenate([ref[...] for ref in row_refs], axis=0)
    width = out_ref.shape[2]
    for part in range(out_ref.shape[0]):
        for column in range(0, width, tile):
            at = part * width + column
            out_ref[part, :, column : column + tile] = dot(
                rows, weight_ref[:, at : at + tile]
            )


def project_more_kernel(tile, own, *refs):
    *row_refs, weight_ref, before_ref, out_ref = refs
    core = lax.axis_index("tensor") % 2
    part = core if own else 1 - core
    rows = jnp.concatenate([ref[...] for ref in row_refs], axis=0)
    width = out_ref.shape[1]
    for column in range(0, width, tile):
        value = before_ref[part, :, column : column + tile] + dot(
            rows, weight_ref[:, column : column + tile]
        )
        out_ref[:, column : column + tile] = value


def split_kernel(own_ref, other_ref, *refs):
    chip = lax.axis_index("tensor") // 2
    width = refs[0].shape[1]
    for i, out_ref in enumerate(refs):
        part = chip if i >= PARTS else 1 - chip
        at = pl.ds(pl.multiple_of((part * PARTS + i % PARTS) * width, width), width)
        out_ref[...] = own_ref[:, at] + other_ref[:, at]


def sum_kernel(kept_ref, arrived_ref, out_ref):
    out_ref[...] = (kept_ref[...] + arrived_ref[...]).astype(out_ref.dtype)


def join_kernel(places, *refs):
    pieces = refs[: len(places)]
    out_ref, sems = refs[-2:]
    here = lax.axis_index("tensor")
    core, chip = here % 2, here // 2
    width = pieces[0].shape[1]
    copies = []
    for i, (place, part) in enumerate(places):
        at = 2 * (1 - core if place // 2 else core) + (1 - chip if place % 2 else chip)
        at = pl.ds(pl.multiple_of((at * PARTS + part) * width, width), width)
        copies.append(pltpu.make_async_copy(pieces[i], out_ref.at[0, :, at], sems.at[i]))
    for copy in copies:
        copy.start()
    for copy in copies:
        copy.wait()


def join(places, pieces, before):
    new_count, width = pieces[0].shape
    return pl.pallas_call(
        lambda *refs: join_kernel(places, *refs),
        out_shape=shape((1, new_count, 4 * PARTS * width), BF16),
        in_specs=[IN_VMEM] * len(places) + ([] if before is None else [IN_HBM]),
        out_specs=IN_HBM,
        scratch_shapes=[pltpu.SemaphoreType.DMA((len(places),))],
        input_output_aliases={} if before is None else {len(places): 0},
        compiler_params=pltpu.CompilerParams(vmem_limit_bytes=4 * MIB),
        name="join",
    )(*pieces, *([] if before is None else [before]))


def square_shards(key_value_rows, queries, w_comp, latent_gain, w_up, w_out, replica_order):
    orders = list(itertools.permutations(range(lax.axis_size("rep"))))
    _, new_count, heads, head_size = queries.shape
    _, tokens, all_groups, width = key_value_rows.shape
    latent_width = w_comp.shape[1]
    rows = heads // 2 * new_count

    chunks = 3 if tokens % 48 == 0 else 1
    latent, query, index, pick = call(
        lambda *refs: compress_kernel(chunks, *refs),
        "compress",
        [shape((tokens, latent_width), BF16), shape((rows, head_size), BF16), *[shape((n,), jnp.int32) for n in (1, 2)]],
        [replica_order, key_value_rows, w_comp, latent_gain, queries],
        16,
        scratch=[
            pltpu.SMEM(replica_order.shape, jnp.int32),
            pltpu.VMEM(key_value_rows.shape[1:], BF16),
            pltpu.VMEM(w_comp.shape, BF16),
            pltpu.VMEM(latent_gain.shape, BF16),
            pltpu.VMEM(queries.shape[1:], BF16),
            pltpu.VMEM((width // 128, tokens * all_groups, 128), F32),
            pltpu.VMEM((tokens, all_groups * width), BF16),
            pltpu.SemaphoreType.DMA((3 + chunks + all_groups,)),
        ],
        hbm_in=5,
        smem_out=2,
        cost=cost(0, 0),
    )

    near = cross(latent, 0)
    far = cross(latent, 1)
    second_query = swap(query, "rep", 2)
    (held,) = fetch("fetch_own", True, w_out)
    second_query, held = lax.optimization_barrier((second_query, held))
    (passed,) = call(
        pass_kernel,
        "pass",
        [shape(query.shape, query.dtype)],
        [pick, query, second_query],
        4,
        smem_in=1,
        cost=cost(0, 0),
    )
    beside = swap(latent, "tensor", 1)
    near, far, beside, _ = lax.optimization_barrier((near, far, beside, passed))
    passed = swap(passed, "rep", 1)
    corner = cross(near, 1)
    near, weight = lax.optimization_barrier((near, w_out))
    held_sent, held_kept = fetch("fetch_other", False, weight)
    near_beside = swap(near, "tensor", 1)
    passed, held_sent, far = lax.optimization_barrier((passed, held_sent, far))
    far_beside = swap(far, "tensor", 1)
    choices = [query, second_query, passed]
    *first, query = score_call("score_chip", [latent, beside], w_up, choices, pick)
    corner, first[2] = lax.optimization_barrier((corner, first[2]))
    corner_beside = swap(corner, "tensor", 1)
    second = score_call("score_next", [near, near_beside, far, far_beside], w_up, query)
    third = score_call("score_corner", [corner, corner_beside], w_up, query)
    depth = rows // new_count * head_size
    attended, attended_other = [], []
    for part in range(PARTS):
        (piece,) = call(
            lambda *refs: attend_kernel(part, tokens, *refs),
            "attend",
            [shape((new_count // PARTS, depth), BF16)],
            [*first, *second, *third],
            16,
            scratch=[pltpu.VMEM((rows // PARTS, head_size), F32)],
            cost=cost(0, 0),
        )
        piece, first[2] = lax.optimization_barrier((piece, first[2]))
        attended.append(piece)
        attended_other.append(swap(piece, "seq", 1))
    columns = w_out.shape[1]
    tile = min(512, columns // 2)
    (partial,) = call(
        lambda *refs: project_kernel(tile, *refs),
        "project",
        [shape((2, new_count, columns // 2), F32)],
        [*attended, held],
        12,
        cost=cost(0, 0),
    )

    def project_more(own, name, weight):
        return call(
            lambda *refs: project_more_kernel(tile, own, *refs),
            name,
            [shape((new_count, columns // 2), F32)],
            [*attended_other, weight, partial],
            12,
            cost=cost(0, 0),
        )[0]

    sent = swap(project_more(False, "project_sent", held_sent), "tensor", 1)
    kept = project_more(True, "project_own", held_kept)
    chunk = (new_count, columns // (4 * PARTS))
    pieces = call(split_kernel, "split", [shape(chunk, F32)] * (2 * PARTS), [kept, sent], 8, cost=cost(0, 0))
    given = [swap(piece, "tensor", 2) for piece in pieces[:PARTS]]
    own, across, beside = [], [], []
    for part in range(PARTS):
        operands = [pieces[PARTS + part], given[part]]
        (summed,) = call(sum_kernel, "sum", [shape(chunk, BF16)], operands, 8, cost=cost(0, 0))
        own.append(route(summed, index[0], orders, True))
        across.append(swap(own[part], "tensor", 2))
        beside.append(swap(own[part], "tensor", 1))
    corners = [swap(across[0], "tensor", 1)]
    joined = join(((0, 0), (2, 0), (0, 1), (1, 0)), [own[0], beside[0], own[1], across[0]], None)
    across[1], joined = lax.optimization_barrier((across[1], joined))
    corners.append(swap(across[1], "tensor", 1))
    joined = join(((2, 1), (1, 1), (3, 0)), [beside[1], across[1], corners[0]], joined)
    return join(((3, 1),), [corners[1]], joined)


def shards(key_value_rows, queries, w_comp, latent_gain, w_up, w_out, replica_order):
    orders = list(itertools.permutations(range(lax.axis_size("rep"))))
    index = order_index(replica_order, orders)
    query = route(queries[0], index, orders, False)
    rows = key_value_rows[0]
    latent = compress(rows.reshape(rows.shape[0], -1), w_comp, latent_gain)
    latent = lax.all_gather(latent, "tensor", axis=0, tiled=True)
    groups = w_up.shape[0]
    lifted = jnp.einsum("tf,gfy->tgy", latent, w_up, preferred_element_type=F32).astype(BF16)
    head_size = query.shape[-1]
    new_count = query.shape[0]
    keys = lifted[..., :head_size]
    values = lifted[..., head_size:]
    grouped_heads = query.reshape(new_count, groups, -1, head_size)
    scores = jnp.einsum(
        "nghd,tgd->nght", grouped_heads, keys, preferred_element_type=F32
    ) * head_size ** (-0.5)
    top = lax.pmax(jnp.max(scores, axis=-1), "seq")
    expo = jnp.exp(scores - top[..., None])
    total = jnp.sum(expo, axis=-1)
    summed = jnp.einsum("nght,tgd->nghd", expo.astype(BF16), values, preferred_element_type=F32)
    summed, total = lax.psum((summed, total), "seq")
    attended = (summed / total[..., None]).astype(BF16).reshape(new_count, -1)
    attended = route(attended, index, orders, True)
    return lax.psum(dot(attended, w_out), "tensor").astype(BF16)[None]


def solution(mesh):
    placed = (
        P("rep", ("seq", "tensor"), None, None),
        P("rep", None, "tensor", None),
        P(),
        P(),
        P("tensor", None, None),
        P("tensor", "seq"),
        P(),
    )
    square = all(mesh.shape[axis] == size for axis, size in (("seq", 2), ("rep", 4), ("tensor", 4)))
    return jax.shard_map(
        square_shards if square else shards,
        mesh=mesh,
        in_specs=placed,
        out_specs=P("rep", None, "seq"),
        check_vma=False,
    )
```

profile of v0, /device:TPU:27, one launch (start us, length us, event | category | flops | bytes accessed | tf_op | source)
XLA Modules:
  0.0 65.6 jit_solution(16864856371306764908)
XLA Ops:
  0.0 3.8 %compress.1 = (bf16[384,512]{1,0:T(8,128)(2,1)S(1)}, bf16[512,128]{1,0:T(8,128)(2,1)S(1)}, s32[1]{0:T(128)}, s32[2]{0:T(128)S(1)}) custom-call(s32[4]{0:T(128)} %refs_0_.2, bf16[1,384,8,256]{3,2,1,0:T(8,128)(2,1)} %refs_1_.1, bf16[2048,512]{1,0:T(8,128)(2,1)} %refs_2_.2, bf16[512]{0:T(512)(128)(2,1)} %refs_3_.2, bf16[1,64,16,128]{3,2,1,0:T(8,128)(2,1)} %refs_4_.2), custom_call_target="tpu_custom_call" | custom-call | tf_op jit(solution)/shard_map/compress/pallas_call | solution.py:32
  3.8 0.3 collective-permute-start.48
  4.1 1.2 %collective-permute-start.49 = (bf16[384,512]{1,0:T(8,128)(2,1)S(1)}, bf16[384,512]{1,0:T(8,128)(2,1)S(1)}, u32[]{:S(2)}, u32[]{:S(2)}) collective-permute-start(bf16[384,512]{1,0:T(8,128)(2,1)S(1)} %get-tuple-element.142.refs_1_), channel_id=1, source_target_pairs={{0,2},{1,17},{2,0},{3,19},{16,18},{17,1},{18,16},{19,3},{4,6},{5,2... | collective-permute-start | bytes 1179656 | tf_op jit(solution)/shard_map/ppermute | solution.py:87
  5.3 1.2 %collective-permute-start.50 = (bf16[384,512]{1,0:T(8,128)(2,1)S(1)}, bf16[384,512]{1,0:T(8,128)(2,1)S(1)}, u32[]{:S(2)}, u32[]{:S(2)}) collective-permute-start(bf16[384,512]{1,0:T(8,128)(2,1)S(1)} %get-tuple-element.142.refs_1_), channel_id=1, source_target_pairs={{0,1},{1,0},{2,3},{3,2},{4,5},{5,4},{6,7},{7,6},{8,9},{9,8},{10,11... | collective-permute-start | bytes 1179656 | tf_op jit(solution)/shard_map/ppermute | solution.py:82
  6.6 0.1 collective-permute-start.51
  6.6 3.5 %fetch_own.1.refs_2_ = bf16[1024,4096]{1,0:T(8,128)(2,1)S(1)} custom-call(bf16[2048,4096]{1,0:T(8,128)(2,1)} %refs_0_.4), custom_call_target="tpu_custom_call" | custom-call | tf_op jit(solution)/shard_map/fetch_own/pallas_call | solution.py:32
  10.1 5.5 %collective-permute-done.51.second_ref.refs_5_ = bf16[512,128]{1,0:T(8,128)(2,1)S(1)} collective-permute-done((bf16[512,128]{1,0:T(8,128)(2,1)S(1)}, bf16[512,128]{1,0:T(8,128)(2,1)S(1)}, u32[]{:S(2)}, u32[]{:S(2)}) %collective-permute-start.51) | collective-permute-done | bytes 131104 | tf_op jit(solution)/shard_map/ppermute | solution.py:82
  15.6 0.6 pass.1
  16.2 0.0 copy-start
  16.3 0.3 collective-permute-start.53
  16.6 3.5 %fetch_other.1 = (bf16[1024,2048]{1,0:T(8,128)(2,1)S(1)}, bf16[1024,2048]{1,0:T(8,128)(2,1)S(1)}) custom-call(bf16[2048,4096]{1,0:T(8,128)(2,1)} %refs_0_.4), custom_call_target="tpu_custom_call" | custom-call | tf_op jit(solution)/shard_map/fetch_other/pallas_call | solution.py:32
  20.1 0.6 collective-permute-done.52.refs_6_
  20.7 2.6 %collective-permute-start.54 = (bf16[384,512]{1,0:T(8,128)(2,1)S(1)}, bf16[384,512]{1,0:T(8,128)(2,1)S(1)}, u32[]{:S(2)}, u32[]{:S(2)}) collective-permute-start(bf16[384,512]{1,0:T(8,128)(2,1)S(1)} %collective-permute-done.48.refs_0_), channel_id=1, source_target_pairs={{0,1},{1,0},{2,3},{3,2},{4,5},{5,4},{6,7},{7,6},{8,9},{9,8},{10,11... | collective-permute-start | bytes 1179656 | tf_op jit(solution)/shard_map/ppermute | solution.py:82
  23.2 1.4 %score_chip.1 = (f32[768,512]{1,0:T(8,128)S(1)}, bf16[768,128]{1,0:T(8,128)(2,1)S(1)}, f32[8,512]{1,0:T(8,128)S(1)}, bf16[512,128]{1,0:T(8,128)(2,1)S(1)}) custom-call(s32[2]{0:T(128)S(1)} %get-tuple-element.141.pick_ref.refs_0_, bf16[384,512]{1,0:T(8,128)(2,1)S(1)} %get-tuple-element.142.refs_1_, bf16[384,512]{1,0:T(8,128)(2,1)S(1)} %collective-permute-done.50.refs_2_, ...), custom_call_target="tpu_custom_call" | custom-call | tf_op jit(solution)/shard_map/score_chip/pallas_call | solution.py:32
  24.6 0.6 collective-permute-start.56
  25.2 1.2 %score_next.1 = (f32[1536,512]{1,0:T(8,128)S(1)}, bf16[1536,128]{1,0:T(8,128)(2,1)S(1)}, f32[8,512]{1,0:T(8,128)S(1)}) custom-call(bf16[384,512]{1,0:T(8,128)(2,1)S(1)} %collective-permute-done.48.refs_0_, bf16[384,512]{1,0:T(8,128)(2,1)S(1)} %collective-permute-done.54.refs_1_, bf16[384,512]{1,0:T(8,128)(2,1)S(1)} %collective-permute-done.49.refs_2_, ...), custom_call_target="tpu_custom_call" | custom-call | tf_op jit(solution)/shard_map/score_next/pallas_call | solution.py:32
  26.4 0.1 collective-permute-done.56.refs_1_
  26.5 0.8 %score_corner.1 = (f32[768,512]{1,0:T(8,128)S(1)}, bf16[768,128]{1,0:T(8,128)(2,1)S(1)}, f32[8,512]{1,0:T(8,128)S(1)}) custom-call(bf16[384,512]{1,0:T(8,128)(2,1)S(1)} %collective-permute-done.53.refs_0_, bf16[384,512]{1,0:T(8,128)(2,1)S(1)} %collective-permute-done.56.refs_1_, bf16[2,512,256]{2,1,0:T(8,128)(2,1)S(1)} %copy-done, ...), custom_call_target="tpu_custom_call" | custom-call | tf_op jit(solution)/shard_map/score_corner/pallas_call | solution.py:32
  27.3 0.7 %attend.2.refs_0_ = bf16[32,1024]{1,0:T(8,128)(2,1)S(1)} custom-call(f32[768,512]{1,0:T(8,128)S(1)} %get-tuple-element.151.refs_0_, bf16[768,128]{1,0:T(8,128)(2,1)S(1)} %get-tuple-element.152.refs_1_, f32[8,512]{1,0:T(8,128)S(1)} %get-tuple-element.166.refs_2_, f32[1536,512]{1,0:T(8,128)S(1)} %get-tuple-element.158.refs_3_, ...), custom_call_target="tpu_custom_call" | custom-call | tf_op jit(solution)/shard_map/attend/pallas_call | solution.py:32
  28.1 0.5 collective-permute-start.57
  28.6 0.7 %attend.3.refs_1_ = bf16[32,1024]{1,0:T(8,128)(2,1)S(1)} custom-call(f32[768,512]{1,0:T(8,128)S(1)} %get-tuple-element.151.refs_0_, bf16[768,128]{1,0:T(8,128)(2,1)S(1)} %get-tuple-element.152.refs_1_, f32[8,512]{1,0:T(8,128)S(1)} %get-tuple-element.166.refs_2_, f32[1536,512]{1,0:T(8,128)S(1)} %get-tuple-element.158.refs_3_, ...), custom_call_target="tpu_custom_call" | custom-call | tf_op jit(solution)/shard_map/attend/pallas_call | solution.py:32
  29.4 1.0 %collective-permute-start.58 = (bf16[32,1024]{1,0:T(8,128)(2,1)S(1)}, bf16[32,1024]{1,0:T(8,128)(2,1)S(1)}, u32[]{:S(2)}, u32[]{:S(2)}) collective-permute-start(bf16[32,1024]{1,0:T(8,128)(2,1)S(1)} %attend.3.refs_1_), channel_id=1, source_target_pairs={{0,16},{16,0},{1,17},{17,1},{2,18},{18,2},{3,19},{19,3},{4,20},{20... | collective-permute-start | bytes 196616 | tf_op jit(solution)/shard_map/ppermute | solution.py:82
  30.4 1.6 %project.1.refs_3_ = f32[2,64,2048]{2,1,0:T(8,128)S(1)} custom-call(bf16[32,1024]{1,0:T(8,128)(2,1)S(1)} %attend.2.refs_0_, bf16[32,1024]{1,0:T(8,128)(2,1)S(1)} %attend.3.refs_1_, bf16[1024,4096]{1,0:T(8,128)(2,1)S(1)} %fetch_own.1.refs_2_), custom_call_target="tpu_custom_call" | custom-call | tf_op jit(solution)/shard_map/project/pallas_call | solution.py:32
  32.0 0.8 %collective-permute-done.58.refs_1_ = bf16[32,1024]{1,0:T(8,128)(2,1)S(1)} collective-permute-done((bf16[32,1024]{1,0:T(8,128)(2,1)S(1)}, bf16[32,1024]{1,0:T(8,128)(2,1)S(1)}, u32[]{:S(2)}, u32[]{:S(2)}) %collective-permute-start.58) | collective-permute-done | bytes 65568 | tf_op jit(solution)/shard_map/ppermute | solution.py:82
  32.8 0.8 %project_sent.1 = f32[64,2048]{1,0:T(8,128)S(1)} custom-call(bf16[32,1024]{1,0:T(8,128)(2,1)S(1)} %collective-permute-done.57.refs_0_, bf16[32,1024]{1,0:T(8,128)(2,1)S(1)} %collective-permute-done.58.refs_1_, bf16[1024,2048]{1,0:T(8,128)(2,1)S(1)} %get-tuple-element.170.refs_2_, f32[2,64,2048]{2,1,0:T(8,128)S(1)} %project.1.refs_3_), custom_call_target="tpu_custom_call" | custom-call | tf_op jit(solution)/shard_map/project_sent/pallas_call | solution.py:32
  33.6 1.6 %collective-permute-start.59 = (f32[64,2048]{1,0:T(8,128)S(1)}, f32[64,2048]{1,0:T(8,128)S(1)}, u32[]{:S(2)}, u32[]{:S(2)}) collective-permute-start(f32[64,2048]{1,0:T(8,128)S(1)} %project_sent.1), channel_id=1, source_target_pairs={{0,1},{1,0},{2,3},{3,2},{4,5},{5,4},{6,7},{7,6},{8,9},{9,8},{10,11... | collective-permute-start | bytes 1572872 | tf_op jit(solution)/shard_map/ppermute | solution.py:82
  35.3 0.8 %project_own.1.own_ref = f32[64,2048]{1,0:T(8,128)S(1)} custom-call(bf16[32,1024]{1,0:T(8,128)(2,1)S(1)} %collective-permute-done.57.refs_0_, bf16[32,1024]{1,0:T(8,128)(2,1)S(1)} %collective-permute-done.58.refs_1_, bf16[1024,2048]{1,0:T(8,128)(2,1)S(1)} %get-tuple-element.168.refs_2_, f32[2,64,2048]{2,1,0:T(8,128)S(1)} %project.1.refs_3_), custom_call_target="tpu_custom_call" | custom-call | tf_op jit(solution)/shard_map/project_own/pallas_call | solution.py:32
  36.1 0.7 %collective-permute-done.59.other_ref = f32[64,2048]{1,0:T(8,128)S(1)} collective-permute-done((f32[64,2048]{1,0:T(8,128)S(1)}, f32[64,2048]{1,0:T(8,128)S(1)}, u32[]{:S(2)}, u32[]{:S(2)}) %collective-permute-start.59) | collective-permute-done | bytes 524320 | tf_op jit(solution)/shard_map/ppermute | solution.py:82
  36.8 0.1 split.1
  36.9 1.3 %collective-permute-start.62 = (f32[64,512]{1,0:T(8,128)S(1)}, f32[64,512]{1,0:T(8,128)S(1)}, u32[]{:S(2)}, u32[]{:S(2)}) collective-permute-start(f32[64,512]{1,0:T(8,128)S(1)} %get-tuple-element.174), channel_id=1, source_target_pairs={{0,2},{1,3},{2,0},{3,1},{4,6},{5,7},{6,4},{7,5},{8,10},{9,11},{10,... | collective-permute-start | bytes 393224 | tf_op jit(solution)/shard_map/ppermute | solution.py:82
  38.1 0.3 collective-permute-start.60
  39.1 2.6 %collective-permute-done.62.arrived_ref = f32[64,512]{1,0:T(8,128)S(1)} collective-permute-done((f32[64,512]{1,0:T(8,128)S(1)}, f32[64,512]{1,0:T(8,128)S(1)}, u32[]{:S(2)}, u32[]{:S(2)}) %collective-permute-start.62) | collective-permute-done | bytes 131104 | tf_op jit(solution)/shard_map/ppermute | solution.py:82
  41.7 6.1 %conditional.3 = (bf16[64,512]{1,0:T(8,128)(2,1)}) conditional(s32[]{:T(128)} %bitcast, bf16[64,512]{1,0:T(8,128)(2,1)S(1)} %sum.3, bf16[64,512]{1,0:T(8,128)(2,1)S(1)} %sum.3, bf16[64,512]{1,0:T(8,128)(2,1)S(1)} %sum.3, bf16[64,512]{1,0:T(8,128)(2,1)S(1)} %sum.3, bf16[64,512]{1,0:T(8,128)(2,1)S(1)} %sum.3, ...), branch_computations={%region_24.0_spmd, %region_25.0_spmd, %region_26.0_spmd, %region_2... | conditional | bytes 262192 | solution.py:72
  41.7 1.9 %collective-permute-start.43 = (bf16[64,512]{1,0:T(8,128)(2,1)S(1)}, bf16[64,512]{1,0:T(8,128)(2,1)}, u32[]{:S(2)}, u32[]{:S(2)}) collective-permute-start(bf16[64,512]{1,0:T(8,128)(2,1)S(1)} %param.43), channel_id=1, source_target_pairs={{12,0},{0,4},{8,8},{4,12},{13,1},{1,5},{9,9},{5,13},{14,2},{2,6},{... | collective-permute-start | bytes 196616 | tf_op jit(solution)/shard_map/cond/branch_19_fun/ppermute | solution.py:70
  43.6 4.1 %collective-permute-done.43 = bf16[64,512]{1,0:T(8,128)(2,1)} collective-permute-done((bf16[64,512]{1,0:T(8,128)(2,1)S(1)}, bf16[64,512]{1,0:T(8,128)(2,1)}, u32[]{:S(2)}, u32[]{:S(2)}) %collective-permute-start.43) | collective-permute-done | bytes 65568 | tf_op jit(solution)/shard_map/cond/branch_19_fun/ppermute | solution.py:70
  47.7 3.2 %collective-permute-start.63 = (bf16[64,512]{1,0:T(8,128)(2,1)}, bf16[64,512]{1,0:T(8,128)(2,1)S(1)}, u32[]{:S(2)}, u32[]{:S(2)}) collective-permute-start(bf16[64,512]{1,0:T(8,128)(2,1)} %get-tuple-element.178.refs_0_), channel_id=1, source_target_pairs={{0,1},{1,0},{2,3},{3,2},{4,5},{5,4},{6,7},{7,6},{8,9},{9,8},{10,11... | collective-permute-start | bytes 196616 | tf_op jit(solution)/shard_map/ppermute | solution.py:82
  50.9 1.2 %collective-permute-start.64 = (bf16[64,512]{1,0:T(8,128)(2,1)}, bf16[64,512]{1,0:T(8,128)(2,1)S(1)}, u32[]{:S(2)}, u32[]{:S(2)}) collective-permute-start(bf16[64,512]{1,0:T(8,128)(2,1)} %get-tuple-element.178.refs_0_), channel_id=1, source_target_pairs={{0,2},{1,3},{2,0},{3,1},{4,6},{5,7},{6,4},{7,5},{8,10},{9,11},{10,... | collective-permute-start | bytes 196616 | tf_op jit(solution)/shard_map/ppermute | solution.py:82
  52.1 6.1 %conditional.2 = (bf16[64,512]{1,0:T(8,128)(2,1)}) conditional(s32[]{:T(128)} %bitcast, bf16[64,512]{1,0:T(8,128)(2,1)S(1)} %sum.2, bf16[64,512]{1,0:T(8,128)(2,1)S(1)} %sum.2, bf16[64,512]{1,0:T(8,128)(2,1)S(1)} %sum.2, bf16[64,512]{1,0:T(8,128)(2,1)S(1)} %sum.2, bf16[64,512]{1,0:T(8,128)(2,1)S(1)} %sum.2, ...), branch_computations={%region_0.0_spmd, %region_1.0_spmd, %region_2.0_spmd, %region_3.0_... | conditional | bytes 262192 | solution.py:72
  52.2 2.5 %collective-permute-start.19 = (bf16[64,512]{1,0:T(8,128)(2,1)S(1)}, bf16[64,512]{1,0:T(8,128)(2,1)}, u32[]{:S(2)}, u32[]{:S(2)}) collective-permute-start(bf16[64,512]{1,0:T(8,128)(2,1)S(1)} %param.19), channel_id=1, source_target_pairs={{12,0},{0,4},{8,8},{4,12},{13,1},{1,5},{9,9},{5,13},{14,2},{2,6},{... | collective-permute-start | bytes 196616 | tf_op jit(solution)/shard_map/cond/branch_19_fun/ppermute | solution.py:70
  54.7 3.5 %collective-permute-done.19 = bf16[64,512]{1,0:T(8,128)(2,1)} collective-permute-done((bf16[64,512]{1,0:T(8,128)(2,1)S(1)}, bf16[64,512]{1,0:T(8,128)(2,1)}, u32[]{:S(2)}, u32[]{:S(2)}) %collective-permute-start.19) | collective-permute-done | bytes 65568 | tf_op jit(solution)/shard_map/cond/branch_19_fun/ppermute | solution.py:70
  58.2 0.2 collective-permute-start.61
  58.4 1.7 %collective-permute-start.66 = (bf16[64,512]{1,0:T(8,128)(2,1)}, bf16[64,512]{1,0:T(8,128)(2,1)S(1)}, u32[]{:S(2)}, u32[]{:S(2)}) collective-permute-start(bf16[64,512]{1,0:T(8,128)(2,1)} %get-tuple-element.177.refs_2_), channel_id=1, source_target_pairs={{0,1},{1,0},{2,3},{3,2},{4,5},{5,4},{6,7},{7,6},{8,9},{9,8},{10,11... | collective-permute-start | bytes 196616 | tf_op jit(solution)/shard_map/ppermute | solution.py:82
  60.1 0.0 collective-permute-start.67
  60.1 1.6 %join.3.refs_3_ = bf16[1,64,4096]{2,1,0:T(8,128)(2,1)} custom-call(bf16[64,512]{1,0:T(8,128)(2,1)} %get-tuple-element.178.refs_0_, bf16[64,512]{1,0:T(8,128)(2,1)S(1)} %collective-permute-done.63.refs_1_, bf16[64,512]{1,0:T(8,128)(2,1)} %get-tuple-element.177.refs_2_, bf16[64,512]{1,0:T(8,128)(2,1)S(1)} %collective-permute-done.64.refs_3_), custom_call_target="tpu_custom_call" | custom-call | tf_op jit(solution)/shard_map/join/pallas_call | solution.py:329
  61.8 2.3 %collective-permute-start.65 = (bf16[64,512]{1,0:T(8,128)(2,1)S(1)}, bf16[64,512]{1,0:T(8,128)(2,1)S(1)}, u32[]{:S(2)}, u32[]{:S(2)}) collective-permute-start(bf16[64,512]{1,0:T(8,128)(2,1)S(1)} %collective-permute-done.61.refs_1_), channel_id=1, source_target_pairs={{0,1},{1,0},{2,3},{3,2},{4,5},{5,4},{6,7},{7,6},{8,9},{9,8},{10,11... | collective-permute-start | bytes 196616 | tf_op jit(solution)/shard_map/ppermute | solution.py:82
  64.1 0.7 %join.4.refs_1_ = bf16[1,64,4096]{2,1,0:T(8,128)(2,1)} custom-call(bf16[64,512]{1,0:T(8,128)(2,1)S(1)} %collective-permute-done.66.refs_0_, bf16[64,512]{1,0:T(8,128)(2,1)S(1)} %collective-permute-done.61.refs_1_, bf16[64,512]{1,0:T(8,128)(2,1)S(1)} %collective-permute-done.67.refs_2_, bf16[1,64,4096]{2,1,0:T(8,128)(2,1)} %join.3.refs_3_), custom_call_target="tpu_custom_call", output_to_operand_aliasing={{}: (3, {})} | custom-call | tf_op jit(solution)/shard_map/join/pallas_call | solution.py:329
  64.8 0.2 collective-permute-done.65.refs_0_
  65.0 0.6 join.5
  (18 shorter events, 0.1 us)
Async XLA Ops:
  3.8 12.4 %collective-permute-start.48 = (bf16[384,512]{1,0:T(8,128)(2,1)S(1)}, bf16[384,512]{1,0:T(8,128)(2,1)S(1)}, u32[]{:S(2)}, u32[]{:S(2)}) collective-permute-start(bf16[384,512]{1,0:T(8,128)(2,1)S(1)} %get-tuple-element.142.refs_1_), channel_id=1, source_target_pairs={{0,16},{1,3},{2,18},{3,1},{16,0},{17,19},{18,2},{19,17},{4,20},{5,... | collective-permute-start | bytes 1179656 | tf_op jit(solution)/shard_map/ppermute | solution.py:87
  4.1 12.1 %collective-permute-start.49 = (bf16[384,512]{1,0:T(8,128)(2,1)S(1)}, bf16[384,512]{1,0:T(8,128)(2,1)S(1)}, u32[]{:S(2)}, u32[]{:S(2)}) collective-permute-start(bf16[384,512]{1,0:T(8,128)(2,1)S(1)} %get-tuple-element.142.refs_1_), channel_id=1, source_target_pairs={{0,2},{1,17},{2,0},{3,19},{16,18},{17,1},{18,16},{19,3},{4,6},{5,2... | collective-permute-start | bytes 1179656 | tf_op jit(solution)/shard_map/ppermute | solution.py:87
  5.3 10.9 %collective-permute-start.50 = (bf16[384,512]{1,0:T(8,128)(2,1)S(1)}, bf16[384,512]{1,0:T(8,128)(2,1)S(1)}, u32[]{:S(2)}, u32[]{:S(2)}) collective-permute-start(bf16[384,512]{1,0:T(8,128)(2,1)S(1)} %get-tuple-element.142.refs_1_), channel_id=1, source_target_pairs={{0,1},{1,0},{2,3},{3,2},{4,5},{5,4},{6,7},{7,6},{8,9},{9,8},{10,11... | collective-permute-start | bytes 1179656 | tf_op jit(solution)/shard_map/ppermute | solution.py:82
  6.6 9.1 %collective-permute-start.51 = (bf16[512,128]{1,0:T(8,128)(2,1)S(1)}, bf16[512,128]{1,0:T(8,128)(2,1)S(1)}, u32[]{:S(2)}, u32[]{:S(2)}) collective-permute-start(bf16[512,128]{1,0:T(8,128)(2,1)S(1)} %get-tuple-element.143.own_ref.refs_4_), channel_id=1, source_target_pairs={{0,8},{4,12},{8,0},{12,4},{1,9},{5,13},{9,1},{13,5},{2,10},{6,14},... | collective-permute-start | bytes 393224 | tf_op jit(solution)/shard_map/ppermute | solution.py:82
  16.2 7.0 %copy-start = (bf16[2,512,256]{2,1,0:T(8,128)(2,1)S(1)}, bf16[2,512,256]{2,1,0:T(8,128)(2,1)}, u32[]{:S(2)}) copy-start(bf16[2,512,256]{2,1,0:T(8,128)(2,1)} %refs_2_.3) | copy-start | bytes 1572868
  16.3 8.3 %collective-permute-start.53 = (bf16[384,512]{1,0:T(8,128)(2,1)S(1)}, bf16[384,512]{1,0:T(8,128)(2,1)S(1)}, u32[]{:S(2)}, u32[]{:S(2)}) collective-permute-start(bf16[384,512]{1,0:T(8,128)(2,1)S(1)} %collective-permute-done.48.refs_0_), channel_id=1, source_target_pairs={{0,2},{1,17},{2,0},{3,19},{16,18},{17,1},{18,16},{19,3},{4,6},{5,2... | collective-permute-start | bytes 1179656 | tf_op jit(solution)/shard_map/ppermute | solution.py:87
  16.5 4.1 %collective-permute-start.52 = (bf16[512,128]{1,0:T(8,128)(2,1)S(1)}, bf16[512,128]{1,0:T(8,128)(2,1)S(1)}, u32[]{:S(2)}, u32[]{:S(2)}) collective-permute-start(bf16[512,128]{1,0:T(8,128)(2,1)S(1)} %pass.1), channel_id=1, source_target_pairs={{0,4},{4,0},{8,12},{12,8},{1,5},{5,1},{9,13},{13,9},{2,6},{6,2},{1... | collective-permute-start | bytes 393224 | tf_op jit(solution)/shard_map/ppermute | solution.py:82
  20.7 4.5 %collective-permute-start.54 = (bf16[384,512]{1,0:T(8,128)(2,1)S(1)}, bf16[384,512]{1,0:T(8,128)(2,1)S(1)}, u32[]{:S(2)}, u32[]{:S(2)}) collective-permute-start(bf16[384,512]{1,0:T(8,128)(2,1)S(1)} %collective-permute-done.48.refs_0_), channel_id=1, source_target_pairs={{0,1},{1,0},{2,3},{3,2},{4,5},{5,4},{6,7},{7,6},{8,9},{9,8},{10,11... | collective-permute-start | bytes 1179656 | tf_op jit(solution)/shard_map/ppermute | solution.py:82
  23.2 2.0 %collective-permute-start.55 = (bf16[384,512]{1,0:T(8,128)(2,1)S(1)}, bf16[384,512]{1,0:T(8,128)(2,1)S(1)}, u32[]{:S(2)}, u32[]{:S(2)}) collective-permute-start(bf16[384,512]{1,0:T(8,128)(2,1)S(1)} %collective-permute-done.49.refs_2_), channel_id=1, source_target_pairs={{0,1},{1,0},{2,3},{3,2},{4,5},{5,4},{6,7},{7,6},{8,9},{9,8},{10,11... | collective-permute-start | bytes 1179656 | tf_op jit(solution)/shard_map/ppermute | solution.py:82
  24.6 1.9 %collective-permute-start.56 = (bf16[384,512]{1,0:T(8,128)(2,1)S(1)}, bf16[384,512]{1,0:T(8,128)(2,1)S(1)}, u32[]{:S(2)}, u32[]{:S(2)}) collective-permute-start(bf16[384,512]{1,0:T(8,128)(2,1)S(1)} %collective-permute-done.53.refs_0_), channel_id=1, source_target_pairs={{0,1},{1,0},{2,3},{3,2},{4,5},{5,4},{6,7},{7,6},{8,9},{9,8},{10,11... | collective-permute-start | bytes 1179656 | tf_op jit(solution)/shard_map/ppermute | solution.py:82
  28.1 3.9 %collective-permute-start.57 = (bf16[32,1024]{1,0:T(8,128)(2,1)S(1)}, bf16[32,1024]{1,0:T(8,128)(2,1)S(1)}, u32[]{:S(2)}, u32[]{:S(2)}) collective-permute-start(bf16[32,1024]{1,0:T(8,128)(2,1)S(1)} %attend.2.refs_0_), channel_id=1, source_target_pairs={{0,16},{16,0},{1,17},{17,1},{2,18},{18,2},{3,19},{19,3},{4,20},{20... | collective-permute-start | bytes 196616 | tf_op jit(solution)/shard_map/ppermute | solution.py:82
  29.4 3.4 %collective-permute-start.58 = (bf16[32,1024]{1,0:T(8,128)(2,1)S(1)}, bf16[32,1024]{1,0:T(8,128)(2,1)S(1)}, u32[]{:S(2)}, u32[]{:S(2)}) collective-permute-start(bf16[32,1024]{1,0:T(8,128)(2,1)S(1)} %attend.3.refs_1_), channel_id=1, source_target_pairs={{0,16},{16,0},{1,17},{17,1},{2,18},{18,2},{3,19},{19,3},{4,20},{20... | collective-permute-start | bytes 196616 | tf_op jit(solution)/shard_map/ppermute | solution.py:82
  33.6 3.2 %collective-permute-start.59 = (f32[64,2048]{1,0:T(8,128)S(1)}, f32[64,2048]{1,0:T(8,128)S(1)}, u32[]{:S(2)}, u32[]{:S(2)}) collective-permute-start(f32[64,2048]{1,0:T(8,128)S(1)} %project_sent.1), channel_id=1, source_target_pairs={{0,1},{1,0},{2,3},{3,2},{4,5},{5,4},{6,7},{7,6},{8,9},{9,8},{10,11... | collective-permute-start | bytes 1572872 | tf_op jit(solution)/shard_map/ppermute | solution.py:82
  36.9 4.8 %collective-permute-start.62 = (f32[64,512]{1,0:T(8,128)S(1)}, f32[64,512]{1,0:T(8,128)S(1)}, u32[]{:S(2)}, u32[]{:S(2)}) collective-permute-start(f32[64,512]{1,0:T(8,128)S(1)} %get-tuple-element.174), channel_id=1, source_target_pairs={{0,2},{1,3},{2,0},{3,1},{4,6},{5,7},{6,4},{7,5},{8,10},{9,11},{10,... | collective-permute-start | bytes 393224 | tf_op jit(solution)/shard_map/ppermute | solution.py:82
  38.1 14.0 %collective-permute-start.60 = (f32[64,512]{1,0:T(8,128)S(1)}, f32[64,512]{1,0:T(8,128)S(1)}, u32[]{:S(2)}, u32[]{:S(2)}) collective-permute-start(f32[64,512]{1,0:T(8,128)S(1)} %get-tuple-element.172), channel_id=1, source_target_pairs={{0,2},{1,3},{2,0},{3,1},{4,6},{5,7},{6,4},{7,5},{8,10},{9,11},{10,... | collective-permute-start | bytes 393224 | tf_op jit(solution)/shard_map/ppermute | solution.py:82
  41.7 6.0 %collective-permute-start.43 = (bf16[64,512]{1,0:T(8,128)(2,1)S(1)}, bf16[64,512]{1,0:T(8,128)(2,1)}, u32[]{:S(2)}, u32[]{:S(2)}) collective-permute-start(bf16[64,512]{1,0:T(8,128)(2,1)S(1)} %param.43), channel_id=1, source_target_pairs={{12,0},{0,4},{8,8},{4,12},{13,1},{1,5},{9,9},{5,13},{14,2},{2,6},{... | collective-permute-start | bytes 196616 | tf_op jit(solution)/shard_map/cond/branch_19_fun/ppermute | solution.py:70
  47.7 12.4 %collective-permute-start.63 = (bf16[64,512]{1,0:T(8,128)(2,1)}, bf16[64,512]{1,0:T(8,128)(2,1)S(1)}, u32[]{:S(2)}, u32[]{:S(2)}) collective-permute-start(bf16[64,512]{1,0:T(8,128)(2,1)} %get-tuple-element.178.refs_0_), channel_id=1, source_target_pairs={{0,1},{1,0},{2,3},{3,2},{4,5},{5,4},{6,7},{7,6},{8,9},{9,8},{10,11... | collective-permute-start | bytes 196616 | tf_op jit(solution)/shard_map/ppermute | solution.py:82
  50.9 9.3 %collective-permute-start.64 = (bf16[64,512]{1,0:T(8,128)(2,1)}, bf16[64,512]{1,0:T(8,128)(2,1)S(1)}, u32[]{:S(2)}, u32[]{:S(2)}) collective-permute-start(bf16[64,512]{1,0:T(8,128)(2,1)} %get-tuple-element.178.refs_0_), channel_id=1, source_target_pairs={{0,2},{1,3},{2,0},{3,1},{4,6},{5,7},{6,4},{7,5},{8,10},{9,11},{10,... | collective-permute-start | bytes 196616 | tf_op jit(solution)/shard_map/ppermute | solution.py:82
  52.2 6.0 %collective-permute-start.19 = (bf16[64,512]{1,0:T(8,128)(2,1)S(1)}, bf16[64,512]{1,0:T(8,128)(2,1)}, u32[]{:S(2)}, u32[]{:S(2)}) collective-permute-start(bf16[64,512]{1,0:T(8,128)(2,1)S(1)} %param.19), channel_id=1, source_target_pairs={{12,0},{0,4},{8,8},{4,12},{13,1},{1,5},{9,9},{5,13},{14,2},{2,6},{... | collective-permute-start | bytes 196616 | tf_op jit(solution)/shard_map/cond/branch_19_fun/ppermute | solution.py:70
  58.2 3.6 %collective-permute-start.61 = (bf16[64,512]{1,0:T(8,128)(2,1)}, bf16[64,512]{1,0:T(8,128)(2,1)S(1)}, u32[]{:S(2)}, u32[]{:S(2)}) collective-permute-start(bf16[64,512]{1,0:T(8,128)(2,1)} %get-tuple-element.177.refs_2_), channel_id=1, source_target_pairs={{0,2},{1,3},{2,0},{3,1},{4,6},{5,7},{6,4},{7,5},{8,10},{9,11},{10,... | collective-permute-start | bytes 196616 | tf_op jit(solution)/shard_map/ppermute | solution.py:82
  58.4 5.7 %collective-permute-start.66 = (bf16[64,512]{1,0:T(8,128)(2,1)}, bf16[64,512]{1,0:T(8,128)(2,1)S(1)}, u32[]{:S(2)}, u32[]{:S(2)}) collective-permute-start(bf16[64,512]{1,0:T(8,128)(2,1)} %get-tuple-element.177.refs_2_), channel_id=1, source_target_pairs={{0,1},{1,0},{2,3},{3,2},{4,5},{5,4},{6,7},{7,6},{8,9},{9,8},{10,11... | collective-permute-start | bytes 196616 | tf_op jit(solution)/shard_map/ppermute | solution.py:82
  60.1 4.0 %collective-permute-start.67 = (bf16[64,512]{1,0:T(8,128)(2,1)S(1)}, bf16[64,512]{1,0:T(8,128)(2,1)S(1)}, u32[]{:S(2)}, u32[]{:S(2)}) collective-permute-start(bf16[64,512]{1,0:T(8,128)(2,1)S(1)} %collective-permute-done.64.refs_3_), channel_id=1, source_target_pairs={{0,1},{1,0},{2,3},{3,2},{4,5},{5,4},{6,7},{7,6},{8,9},{9,8},{10,11... | collective-permute-start | bytes 196616 | tf_op jit(solution)/shard_map/ppermute | solution.py:82
  61.8 3.2 %collective-permute-start.65 = (bf16[64,512]{1,0:T(8,128)(2,1)S(1)}, bf16[64,512]{1,0:T(8,128)(2,1)S(1)}, u32[]{:S(2)}, u32[]{:S(2)}) collective-permute-start(bf16[64,512]{1,0:T(8,128)(2,1)S(1)} %collective-permute-done.61.refs_1_), channel_id=1, source_target_pairs={{0,1},{1,0},{2,3},{3,2},{4,5},{5,4},{6,7},{7,6},{8,9},{9,8},{10,11... | collective-permute-start | bytes 196616 | tf_op jit(solution)/shard_map/ppermute | solution.py:82
where the time goes:
time: 66.4 us; the launch traced here: 65.6 us
  starting transfers between devices  24.2 us (36%)
  Pallas kernels  22.4 us (34%)
  waiting for transfers between devices  18.1 us (27%)
  between operations  0.85 us (1%)
    pallas_call x15, Pallas kernels, call(): pl.pallas_call(body, out_shape=outs, in_specs=specs, out_specs=out_specs,...  19.5 us
    ppermute x17, starting transfers between devices, swap(): return lax.ppermute(value, axis, pairs)  17.9 us
    ppermute x17, waiting for transfers between devices, swap(): return lax.ppermute(value, axis, pairs)  10.6 us
    ppermute x2, waiting for transfers between devices, branch(): return lambda v: lax.ppermute(v, 'rep', route_pairs(order, back))  7.55 us
    ppermute x2, starting transfers between devices, branch(): return lambda v: lax.ppermute(v, 'rep', route_pairs(order, back))  4.46 us
    pallas_call x3, Pallas kernels, join(): pl.pallas_call(lambda *refs: join_kernel(places, *refs), out_shape=shape(...  2.93 us
    ppermute x3, starting transfers between devices, cross(): return lax.ppermute(value, ('seq', 'tensor'), pairs)  1.85 us
  transfers between devices with their start and end apart: 22, of which 9 were waited for; matrix products, arithmetic and copies ran while one was open for 0% of the time, Pallas kernels for 24%

commit v1 on v0

--- a/solution.py
+++ b/solution.py
@@ -14,7 +14,7 @@
 IN_SMEM = pl.BlockSpec(memory_space=pltpu.SMEM)
 IN_HBM = pl.BlockSpec(memory_space=pltpu.HBM)
 COPIES = 8
-PARTS = 2
+PARTS = 1
 
 
 def shape(dims, dtype):
@@ -216,8 +216,11 @@
             out_ref[...] = ref[...]
 
 
-def pass_kernel(pick_ref, own_ref, second_ref, out_ref):
+def pass_kernel(pick_ref, own_ref, second_ref, near_ref, far_ref, out_ref, upper_ref, lower_ref):
     choose(pick_ref[0], (own_ref, second_ref), out_ref)
+    half = upper_ref.shape[0]
+    upper_ref[...] = near_ref[:half]
+    lower_ref[...] = far_ref[half:]
 
 
 def choose_and_score_kernel(parts, pick_ref, *refs):
@@ -294,12 +297,11 @@
         out_ref[:, column : column + tile] = value
 
 
-def split_kernel(own_ref, other_ref, *refs):
+def split_kernel(own_ref, other_ref, given_ref, kept_ref):
     chip = lax.axis_index("tensor") // 2
-    width = refs[0].shape[1]
-    for i, out_ref in enumerate(refs):
-        part = chip if i >= PARTS else 1 - chip
-        at = pl.ds(pl.multiple_of((part * PARTS + i % PARTS) * width, width), width)
+    width = given_ref.shape[1]
+    for out_ref, part in ((given_ref, 1 - chip), (kept_ref, chip)):
+        at = pl.ds(pl.multiple_of(part * width, width), width)
         out_ref[...] = own_ref[:, at] + other_ref[:, at]
 
 
@@ -314,9 +316,9 @@
     core, chip = here % 2, here // 2
     width = pieces[0].shape[1]
     copies = []
-    for i, (place, part) in enumerate(places):
+    for i, place in enumerate(places):
         at = 2 * (1 - core if place // 2 else core) + (1 - chip if place % 2 else chip)
-        at = pl.ds(pl.multiple_of((at * PARTS + part) * width, width), width)
+        at = pl.ds(pl.multiple_of(at * width, width), width)
         copies.append(pltpu.make_async_copy(pieces[i], out_ref.at[0, :, at], sems.at[i]))
     for copy in copies:
         copy.start()
@@ -328,7 +330,7 @@
     new_count, width = pieces[0].shape
     return pl.pallas_call(
         lambda *refs: join_kernel(places, *refs),
-        out_shape=shape((1, new_count, 4 * PARTS * width), BF16),
+        out_shape=shape((1, new_count, 4 * width), BF16),
         in_specs=[IN_VMEM] * len(places) + ([] if before is None else [IN_HBM]),
         out_specs=IN_HBM,
         scratch_shapes=[pltpu.SemaphoreType.DMA((len(places),))],
@@ -371,36 +373,36 @@
     far = cross(latent, 1)
     second_query = swap(query, "rep", 2)
     (held,) = fetch("fetch_own", True, w_out)
-    second_query, held = lax.optimization_barrier((second_query, held))
-    (passed,) = call(
+    near, far, second_query, held = lax.optimization_barrier((near, far, second_query, held))
+    passed, upper, lower = call(
         pass_kernel,
         "pass",
-        [shape(query.shape, query.dtype)],
-        [pick, query, second_query],
+        [shape(query.shape, query.dtype)] + [shape((tokens // 2, latent_width), BF16)] * 2,
+        [pick, query, second_query, near, far],
         4,
         smem_in=1,
         cost=cost(0, 0),
     )
-    beside = swap(latent, "tensor", 1)
-    near, far, beside, _ = lax.optimization_barrier((near, far, beside, passed))
+    corner = [cross(upper, 1), cross(lower, 0)]
     passed = swap(passed, "rep", 1)
-    corner = cross(near, 1)
-    near, weight = lax.optimization_barrier((near, w_out))
+    weight, _ = lax.optimization_barrier((w_out, upper))
     held_sent, held_kept = fetch("fetch_other", False, weight)
-    near_beside = swap(near, "tensor", 1)
-    passed, held_sent, far = lax.optimization_barrier((passed, held_sent, far))
-    far_beside = swap(far, "tensor", 1)
+    passed, held_sent, given, near, far = lax.optimization_barrier(
+        (passed, held_sent, latent, near, far)
+    )
+    besides = [swap(piece, "tensor", 1) for piece in (given, near, far)]
     choices = [query, second_query, passed]
-    *first, query = score_call("score_chip", [latent, beside], w_up, choices, pick)
+    *first, query = score_call("score_here", [given, near, far], w_up, choices, pick)
     corner, first[2] = lax.optimization_barrier((corner, first[2]))
-    corner_beside = swap(corner, "tensor", 1)
-    second = score_call("score_next", [near, near_beside, far, far_beside], w_up, query)
-    third = score_call("score_corner", [corner, corner_beside], w_up, query)
+    corner += [swap(piece, "tensor", 1) for piece in corner]
+    second = list(score_call("score_beside", besides, w_up, query))
+    corner[2], second[2] = lax.optimization_barrier((corner[2], second[2]))
+    third = score_call("score_corner", corner, w_up, query)
     depth = rows // new_count * head_size
     attended, attended_other = [], []
     for part in range(PARTS):
         (piece,) = call(
-            lambda *refs: attend_kernel(part, tokens, *refs),
+            lambda *refs, part=part: attend_kernel(part, tokens, *refs),
             "attend",
             [shape((new_count // PARTS, depth), BF16)],
             [*first, *second, *third],
@@ -434,22 +436,18 @@
 
     sent = swap(project_more(False, "project_sent", held_sent), "tensor", 1)
     kept = project_more(True, "project_own", held_kept)
-    chunk = (new_count, columns // (4 * PARTS))
-    pieces = call(split_kernel, "split", [shape(chunk, F32)] * (2 * PARTS), [kept, sent], 8, cost=cost(0, 0))
-    given = [swap(piece, "tensor", 2) for piece in pieces[:PARTS]]
-    own, across, beside = [], [], []
-    for part in range(PARTS):
-        operands = [pieces[PARTS + part], given[part]]
-        (summed,) = call(sum_kernel, "sum", [shape(chunk, BF16)], operands, 8, cost=cost(0, 0))
-        own.append(route(summed, index[0], orders, True))
-        across.append(swap(own[part], "tensor", 2))
-        beside.append(swap(own[part], "tensor", 1))
-    corners = [swap(across[0], "tensor", 1)]
-    joined = join(((0, 0), (2, 0), (0, 1), (1, 0)), [own[0], beside[0], own[1], across[0]], None)
-    across[1], joined = lax.optimization_barrier((across[1], joined))
-    corners.append(swap(across[1], "tensor", 1))
-    joined = join(((2, 1), (1, 1), (3, 0)), [beside[1], across[1], corners[0]], joined)
-    return join(((3, 1),), [corners[1]], joined)
+    quarter = (new_count, columns // 4)
+    given, kept = call(split_kernel, "split", [shape(quarter, F32)] * 2, [kept, sent], 8, cost=cost(0, 0))
+    given = swap(given, "tensor", 2)
+    (own,) = call(sum_kernel, "sum", [shape(quarter, BF16)], [kept, given], 8, cost=cost(0, 0))
+    own = route(own, index[0], orders, True)
+    across = swap(own, "tensor", 2)
+    beside = swap(own, "tensor", 1)
+    joined = join((0, 2), [own, beside], None)
+    across, joined = lax.optimization_barrier((across, joined))
+    last = swap(across, "tensor", 1)
+    joined = join((1,), [across], joined)
+    return join((3,), [last], joined)
 
 
 def shards(key_value_rows, queries, w_comp, latent_gain, w_up, w_out, replica_order):

time: 66.4 us -> 63.8 us (0.961)
  the two profiles are of different devices: /device:TPU:27 before, /device:TPU:17 now
where the time goes in v1:
time: 63.8 us; the launch traced here: 62.6 us
  waiting for transfers between devices  23.5 us (37%)
  Pallas kernels  22.3 us (35%)
  starting transfers between devices  16 us (25%)
  between operations  0.81 us (1%)
    pallas_call x13, Pallas kernels, call(): pl.pallas_call(body, out_shape=outs, in_specs=specs, out_specs=out_specs,...  19.4 us
    ppermute x13, waiting for transfers between devices, swap(): return lax.ppermute(value, axis, pairs)  14.8 us
    ppermute x13, starting transfers between devices, swap(): return lax.ppermute(value, axis, pairs)  10.1 us
    ppermute x4, waiting for transfers between devices, cross(): return lax.ppermute(value, ('seq', 'tensor'), pairs)  4.9 us
    ppermute x4, starting transfers between devices, cross(): return lax.ppermute(value, ('seq', 'tensor'), pairs)  3.74 us
    ppermute x1, waiting for transfers between devices, branch(): return lambda v: lax.ppermute(v, 'rep', route_pairs(order, back))  3.73 us
    pallas_call x3, Pallas kernels, join(): pl.pallas_call(lambda *refs: join_kernel(places, *refs), out_shape=shape(...  2.94 us
    ppermute x1, starting transfers between devices, branch(): return lambda v: lax.ppermute(v, 'rep', route_pairs(order, back))  2.08 us
  transfers between devices with their start and end apart: 18, of which 11 were waited for; matrix products, arithmetic and copies ran while one was open for 0% of the time, Pallas kernels for 23%

profile of v1, /device:TPU:17, one launch (start us, length us, event | category | flops | bytes accessed | tf_op | source)
XLA Modules:
  0.0 62.6 jit_solution(3025386933374803455)
XLA Ops:
  0.0 3.8 %compress.1 = (bf16[384,512]{1,0:T(8,128)(2,1)S(1)}, bf16[512,128]{1,0:T(8,128)(2,1)S(1)}, s32[1]{0:T(128)}, s32[2]{0:T(128)S(1)}) custom-call(s32[4]{0:T(128)} %refs_0_.2, bf16[1,384,8,256]{3,2,1,0:T(8,128)(2,1)} %refs_1_.1, bf16[2048,512]{1,0:T(8,128)(2,1)} %refs_2_.1, bf16[512]{0:T(512)(128)(2,1)} %refs_3_.2, bf16[1,64,16,128]{3,2,1,0:T(8,128)(2,1)} %refs_4_.3), custom_call_target="tpu_custom_call" | custom-call | tf_op jit(solution)/shard_map/compress/pallas_call | solution.py:32
  3.8 1.3 %collective-permute-start.25 = (bf16[384,512]{1,0:T(8,128)(2,1)S(1)}, bf16[384,512]{1,0:T(8,128)(2,1)S(1)}, u32[]{:S(2)}, u32[]{:S(2)}) collective-permute-start(bf16[384,512]{1,0:T(8,128)(2,1)S(1)} %get-tuple-element.104.refs_1_), channel_id=1, source_target_pairs={{0,2},{1,17},{2,0},{3,19},{16,18},{17,1},{18,16},{19,3},{4,6},{5,2... | collective-permute-start | bytes 1179656 | tf_op jit(solution)/shard_map/ppermute | solution.py:87
  5.1 1.2 %collective-permute-start.24 = (bf16[384,512]{1,0:T(8,128)(2,1)S(1)}, bf16[384,512]{1,0:T(8,128)(2,1)S(1)}, u32[]{:S(2)}, u32[]{:S(2)}) collective-permute-start(bf16[384,512]{1,0:T(8,128)(2,1)S(1)} %get-tuple-element.104.refs_1_), channel_id=1, source_target_pairs={{0,16},{1,3},{2,18},{3,1},{16,0},{17,19},{18,2},{19,17},{4,20},{5,... | collective-permute-start | bytes 1179656 | tf_op jit(solution)/shard_map/ppermute | solution.py:87
  6.3 0.1 collective-permute-start.26
  6.4 3.5 %fetch_own.1.refs_1_ = bf16[1024,4096]{1,0:T(8,128)(2,1)S(1)} custom-call(bf16[2048,4096]{1,0:T(8,128)(2,1)} %refs_0_.4), custom_call_target="tpu_custom_call" | custom-call | tf_op jit(solution)/shard_map/fetch_own/pallas_call | solution.py:32
  9.8 1.3 %collective-permute-done.26.second_ref.refs_6_ = bf16[512,128]{1,0:T(8,128)(2,1)S(1)} collective-permute-done((bf16[512,128]{1,0:T(8,128)(2,1)S(1)}, bf16[512,128]{1,0:T(8,128)(2,1)S(1)}, u32[]{:S(2)}, u32[]{:S(2)}) %collective-permute-start.26) | collective-permute-done | bytes 131104 | tf_op jit(solution)/shard_map/ppermute | solution.py:82
  11.1 1.2 %collective-permute-done.25.far_ref.refs_3_ = bf16[384,512]{1,0:T(8,128)(2,1)S(1)} collective-permute-done((bf16[384,512]{1,0:T(8,128)(2,1)S(1)}, bf16[384,512]{1,0:T(8,128)(2,1)S(1)}, u32[]{:S(2)}, u32[]{:S(2)}) %collective-permute-start.25) | collective-permute-done | bytes 393248 | tf_op jit(solution)/shard_map/ppermute | solution.py:87
  12.3 3.7 %collective-permute-done.24.near_ref.refs_2_ = bf16[384,512]{1,0:T(8,128)(2,1)S(1)} collective-permute-done((bf16[384,512]{1,0:T(8,128)(2,1)S(1)}, bf16[384,512]{1,0:T(8,128)(2,1)S(1)}, u32[]{:S(2)}, u32[]{:S(2)}) %collective-permute-start.24) | collective-permute-done | bytes 393248 | tf_op jit(solution)/shard_map/ppermute | solution.py:87
  16.0 0.6 pass.1
  16.6 1.4 %collective-permute-start.27 = (bf16[512,128]{1,0:T(8,128)(2,1)S(1)}, bf16[512,128]{1,0:T(8,128)(2,1)S(1)}, u32[]{:S(2)}, u32[]{:S(2)}) collective-permute-start(bf16[512,128]{1,0:T(8,128)(2,1)S(1)} %get-tuple-element.100), channel_id=1, source_target_pairs={{0,4},{4,0},{8,12},{12,8},{1,5},{5,1},{9,13},{13,9},{2,6},{6,2},{1... | collective-permute-start | bytes 393224 | tf_op jit(solution)/shard_map/ppermute | solution.py:82
  18.0 0.0 collective-permute-start.28
  18.0 1.2 %collective-permute-start.29 = (bf16[192,512]{1,0:T(8,128)(2,1)S(1)}, bf16[192,512]{1,0:T(8,128)(2,1)S(1)}, u32[]{:S(2)}, u32[]{:S(2)}) collective-permute-start(bf16[192,512]{1,0:T(8,128)(2,1)S(1)} %get-tuple-element.110), channel_id=1, source_target_pairs={{0,16},{1,3},{2,18},{3,1},{16,0},{17,19},{18,2},{19,17},{4,20},{5,... | collective-permute-start | bytes 589832 | tf_op jit(solution)/shard_map/ppermute | solution.py:87
  19.2 3.5 %fetch_other.1 = (bf16[1024,2048]{1,0:T(8,128)(2,1)S(1)}, bf16[1024,2048]{1,0:T(8,128)(2,1)S(1)}) custom-call(bf16[2048,4096]{1,0:T(8,128)(2,1)} %refs_0_.4), custom_call_target="tpu_custom_call" | custom-call | tf_op jit(solution)/shard_map/fetch_other/pallas_call | solution.py:32
  22.7 0.0 collective-permute-done.27.refs_7_
  22.7 1.7 %collective-permute-start.30 = (bf16[384,512]{1,0:T(8,128)(2,1)S(1)}, bf16[384,512]{1,0:T(8,128)(2,1)S(1)}, u32[]{:S(2)}, u32[]{:S(2)}) collective-permute-start(bf16[384,512]{1,0:T(8,128)(2,1)S(1)} %get-tuple-element.104.refs_1_), channel_id=1, source_target_pairs={{0,1},{1,0},{2,3},{3,2},{4,5},{5,4},{6,7},{7,6},{8,9},{9,8},{10,11... | collective-permute-start | bytes 1179656 | tf_op jit(solution)/shard_map/ppermute | solution.py:82
  24.4 0.1 collective-permute-start.31
  24.5 0.4 collective-permute-start.32
  25.0 1.6 %score_here.1 = (f32[1152,512]{1,0:T(8,128)S(1)}, bf16[1152,128]{1,0:T(8,128)(2,1)S(1)}, f32[8,512]{1,0:T(8,128)S(1)}, bf16[512,128]{1,0:T(8,128)(2,1)S(1)}) custom-call(s32[2]{0:T(128)S(1)} %get-tuple-element.94.pick_ref.refs_0_, bf16[384,512]{1,0:T(8,128)(2,1)S(1)} %get-tuple-element.104.refs_1_, ...), custom_call_target="tpu_custom_call" | custom-call | tf_op jit(solution)/shard_map/score_here/pallas_call | solution.py:32
  26.5 0.0 collective-permute-done.29.refs_1_
  26.5 0.0 collective-permute-done.28.refs_0_
  26.6 0.1 collective-permute-start.33
  26.7 0.4 collective-permute-start.34
  27.1 1.0 %score_beside.1 = (f32[1152,512]{1,0:T(8,128)S(1)}, bf16[1152,128]{1,0:T(8,128)(2,1)S(1)}, f32[8,512]{1,0:T(8,128)S(1)}) custom-call(bf16[384,512]{1,0:T(8,128)(2,1)S(1)} %collective-permute-done.30.refs_0_, bf16[384,512]{1,0:T(8,128)(2,1)S(1)} %collective-permute-done.31.refs_1_, bf16[384,512]{1,0:T(8,128)(2,1)S(1)} %collective-permute-done.32.refs_2_, ...), custom_call_target="tpu_custom_call" | custom-call | tf_op jit(solution)/shard_map/score_beside/pallas_call | solution.py:32
  28.2 0.2 collective-permute-done.34.refs_3_
  28.3 0.7 %score_corner.1 = (f32[768,512]{1,0:T(8,128)S(1)}, bf16[768,128]{1,0:T(8,128)(2,1)S(1)}, f32[8,512]{1,0:T(8,128)S(1)}) custom-call(bf16[192,512]{1,0:T(8,128)(2,1)S(1)} %collective-permute-done.28.refs_0_, bf16[192,512]{1,0:T(8,128)(2,1)S(1)} %collective-permute-done.29.refs_1_, bf16[192,512]{1,0:T(8,128)(2,1)S(1)} %collective-permute-done.33.refs_2_, ...), custom_call_target="tpu_custom_call" | custom-call | tf_op jit(solution)/shard_map/score_corner/pallas_call | solution.py:32
  29.1 1.4 %attend.1.refs_0_ = bf16[64,1024]{1,0:T(8,128)(2,1)S(1)} custom-call(f32[1152,512]{1,0:T(8,128)S(1)} %get-tuple-element.108.refs_0_, bf16[1152,128]{1,0:T(8,128)(2,1)S(1)} %get-tuple-element.109.refs_1_, f32[8,512]{1,0:T(8,128)S(1)} %get-tuple-element.112.refs_2_, f32[1152,512]{1,0:T(8,128)S(1)} %get-tuple-element.114.refs_3_, ...), custom_call_target="tpu_custom_call" | custom-call | tf_op jit(solution)/shard_map/attend/pallas_call | solution.py:32
  30.5 1.1 %collective-permute-start.35 = (bf16[64,1024]{1,0:T(8,128)(2,1)S(1)}, bf16[64,1024]{1,0:T(8,128)(2,1)S(1)}, u32[]{:S(2)}, u32[]{:S(2)}) collective-permute-start(bf16[64,1024]{1,0:T(8,128)(2,1)S(1)} %attend.1.refs_0_), channel_id=1, source_target_pairs={{0,16},{16,0},{1,17},{17,1},{2,18},{18,2},{3,19},{19,3},{4,20},{20... | collective-permute-start | bytes 393224 | tf_op jit(solution)/shard_map/ppermute | solution.py:82
  31.6 1.5 %project.1.refs_2_ = f32[2,64,2048]{2,1,0:T(8,128)S(1)} custom-call(bf16[64,1024]{1,0:T(8,128)(2,1)S(1)} %attend.1.refs_0_, bf16[1024,4096]{1,0:T(8,128)(2,1)S(1)} %fetch_own.1.refs_1_), custom_call_target="tpu_custom_call" | custom-call | tf_op jit(solution)/shard_map/project/pallas_call | solution.py:32
  33.2 2.3 %collective-permute-done.35.refs_0_ = bf16[64,1024]{1,0:T(8,128)(2,1)S(1)} collective-permute-done((bf16[64,1024]{1,0:T(8,128)(2,1)S(1)}, bf16[64,1024]{1,0:T(8,128)(2,1)S(1)}, u32[]{:S(2)}, u32[]{:S(2)}) %collective-permute-start.35) | collective-permute-done | bytes 131104 | tf_op jit(solution)/shard_map/ppermute | solution.py:82
  35.4 0.8 %project_sent.1 = f32[64,2048]{1,0:T(8,128)S(1)} custom-call(bf16[64,1024]{1,0:T(8,128)(2,1)S(1)} %collective-permute-done.35.refs_0_, bf16[1024,2048]{1,0:T(8,128)(2,1)S(1)} %get-tuple-element.127.refs_1_, f32[2,64,2048]{2,1,0:T(8,128)S(1)} %project.1.refs_2_), custom_call_target="tpu_custom_call" | custom-call | tf_op jit(solution)/shard_map/project_sent/pallas_call | solution.py:32
  36.3 1.1 %collective-permute-start.36 = (f32[64,2048]{1,0:T(8,128)S(1)}, f32[64,2048]{1,0:T(8,128)S(1)}, u32[]{:S(2)}, u32[]{:S(2)}) collective-permute-start(f32[64,2048]{1,0:T(8,128)S(1)} %project_sent.1), channel_id=1, source_target_pairs={{0,1},{1,0},{2,3},{3,2},{4,5},{5,4},{6,7},{7,6},{8,9},{9,8},{10,11... | collective-permute-start | bytes 1572872 | tf_op jit(solution)/shard_map/ppermute | solution.py:82
  37.4 0.8 %project_own.1.own_ref = f32[64,2048]{1,0:T(8,128)S(1)} custom-call(bf16[64,1024]{1,0:T(8,128)(2,1)S(1)} %collective-permute-done.35.refs_0_, bf16[1024,2048]{1,0:T(8,128)(2,1)S(1)} %get-tuple-element.125.refs_1_, f32[2,64,2048]{2,1,0:T(8,128)S(1)} %project.1.refs_2_), custom_call_target="tpu_custom_call" | custom-call | tf_op jit(solution)/shard_map/project_own/pallas_call | solution.py:32
  38.2 0.7 %collective-permute-done.36.other_ref = f32[64,2048]{1,0:T(8,128)S(1)} collective-permute-done((f32[64,2048]{1,0:T(8,128)S(1)}, f32[64,2048]{1,0:T(8,128)S(1)}, u32[]{:S(2)}, u32[]{:S(2)}) %collective-permute-start.36) | collective-permute-done | bytes 524320 | tf_op jit(solution)/shard_map/ppermute | solution.py:82
  38.9 0.1 split.1
  39.0 0.3 collective-permute-start.37
  40.0 6.6 %collective-permute-done.37.arrived_ref = f32[64,1024]{1,0:T(8,128)S(1)} collective-permute-done((f32[64,1024]{1,0:T(8,128)S(1)}, f32[64,1024]{1,0:T(8,128)S(1)}, u32[]{:S(2)}, u32[]{:S(2)}) %collective-permute-start.37) | collective-permute-done | bytes 262176 | tf_op jit(solution)/shard_map/ppermute | solution.py:82
  46.6 5.8 %conditional.1 = (bf16[64,1024]{1,0:T(8,128)(2,1)}) conditional(s32[]{:T(128)} %bitcast, bf16[64,1024]{1,0:T(8,128)(2,1)S(1)} %sum.1, bf16[64,1024]{1,0:T(8,128)(2,1)S(1)} %sum.1, bf16[64,1024]{1,0:T(8,128)(2,1)S(1)} %sum.1, bf16[64,1024]{1,0:T(8,128)(2,1)S(1)} %sum.1, bf16[64,1024]{1,0:T(8,128)(2,1)S(1)} %sum.1, ...), branch_computations={%region_0.0_spmd, %region_1.0_spmd, %region_2.0_spmd, %region_3.0_... | conditional | bytes 524336 | solution.py:72
  46.6 2.1 %collective-permute-start.1 = (bf16[64,1024]{1,0:T(8,128)(2,1)S(1)}, bf16[64,1024]{1,0:T(8,128)(2,1)}, u32[]{:S(2)}, u32[]{:S(2)}) collective-permute-start(bf16[64,1024]{1,0:T(8,128)(2,1)S(1)} %param.1), channel_id=1, source_target_pairs={{0,0},{4,4},{12,8},{8,12},{1,1},{5,5},{13,9},{9,13},{2,2},{6,6},{1... | collective-permute-start | bytes 393224 | tf_op jit(solution)/shard_map/cond/branch_1_fun/ppermute | solution.py:70
  48.7 3.7 %collective-permute-done.1 = bf16[64,1024]{1,0:T(8,128)(2,1)} collective-permute-done((bf16[64,1024]{1,0:T(8,128)(2,1)S(1)}, bf16[64,1024]{1,0:T(8,128)(2,1)}, u32[]{:S(2)}, u32[]{:S(2)}) %collective-permute-start.1) | collective-permute-done | bytes 131104 | tf_op jit(solution)/shard_map/cond/branch_1_fun/ppermute | solution.py:70
  52.5 2.4 %collective-permute-start.39 = (bf16[64,1024]{1,0:T(8,128)(2,1)}, bf16[64,1024]{1,0:T(8,128)(2,1)S(1)}, u32[]{:S(2)}, u32[]{:S(2)}) collective-permute-start(bf16[64,1024]{1,0:T(8,128)(2,1)} %get-tuple-element.132.refs_0_), channel_id=1, source_target_pairs={{0,1},{1,0},{2,3},{3,2},{4,5},{5,4},{6,7},{7,6},{8,9},{9,8},{10,11... | collective-permute-start | bytes 393224 | tf_op jit(solution)/shard_map/ppermute | solution.py:82
  54.8 0.2 collective-permute-start.38
  55.1 0.9 %collective-permute-done.39.refs_1_ = bf16[64,1024]{1,0:T(8,128)(2,1)S(1)} collective-permute-done((bf16[64,1024]{1,0:T(8,128)(2,1)}, bf16[64,1024]{1,0:T(8,128)(2,1)S(1)}, u32[]{:S(2)}, u32[]{:S(2)}) %collective-permute-start.39) | collective-permute-done | bytes 131104 | tf_op jit(solution)/shard_map/ppermute | solution.py:82
  56.0 1.6 %join.3.refs_1_ = bf16[1,64,4096]{2,1,0:T(8,128)(2,1)} custom-call(bf16[64,1024]{1,0:T(8,128)(2,1)} %get-tuple-element.132.refs_0_, bf16[64,1024]{1,0:T(8,128)(2,1)S(1)} %collective-permute-done.39.refs_1_), custom_call_target="tpu_custom_call" | custom-call | tf_op jit(solution)/shard_map/join/pallas_call | solution.py:331
  57.6 2.5 %collective-permute-done.38.refs_0_ = bf16[64,1024]{1,0:T(8,128)(2,1)S(1)} collective-permute-done((bf16[64,1024]{1,0:T(8,128)(2,1)}, bf16[64,1024]{1,0:T(8,128)(2,1)S(1)}, u32[]{:S(2)}, u32[]{:S(2)}) %collective-permute-start.38) | collective-permute-done | bytes 131104 | tf_op jit(solution)/shard_map/ppermute | solution.py:82
  60.1 0.8 %collective-permute-start.40 = (bf16[64,1024]{1,0:T(8,128)(2,1)S(1)}, bf16[64,1024]{1,0:T(8,128)(2,1)S(1)}, u32[]{:S(2)}, u32[]{:S(2)}) collective-permute-start(bf16[64,1024]{1,0:T(8,128)(2,1)S(1)} %collective-permute-done.38.refs_0_), channel_id=1, source_target_pairs={{0,1},{1,0},{2,3},{3,2},{4,5},{5,4},{6,7},{7,6},{8,9},{9,8},{10,11... | collective-permute-start | bytes 393224 | tf_op jit(solution)/shard_map/ppermute | solution.py:82
  60.9 0.7 %join.4.refs_1_ = bf16[1,64,4096]{2,1,0:T(8,128)(2,1)} custom-call(bf16[64,1024]{1,0:T(8,128)(2,1)S(1)} %collective-permute-done.38.refs_0_, bf16[1,64,4096]{2,1,0:T(8,128)(2,1)} %join.3.refs_1_), custom_call_target="tpu_custom_call", output_to_operand_aliasing={{}: (1, {})} | custom-call | tf_op jit(solution)/shard_map/join/pallas_call | solution.py:331
  61.6 0.3 collective-permute-done.40.refs_0_
  61.9 0.7 %join.5 = bf16[1,64,4096]{2,1,0:T(8,128)(2,1)} custom-call(bf16[64,1024]{1,0:T(8,128)(2,1)S(1)} %collective-permute-done.40.refs_0_, bf16[1,64,4096]{2,1,0:T(8,128)(2,1)} %join.4.refs_1_), custom_call_target="tpu_custom_call", output_to_operand_aliasing={{}: (1, {})} | custom-call | tf_op jit(solution)/shard_map/join/pallas_call | solution.py:331
  (7 shorter events, 0.0 us)
Async XLA Ops:
  3.8 8.5 %collective-permute-start.25 = (bf16[384,512]{1,0:T(8,128)(2,1)S(1)}, bf16[384,512]{1,0:T(8,128)(2,1)S(1)}, u32[]{:S(2)}, u32[]{:S(2)}) collective-permute-start(bf16[384,512]{1,0:T(8,128)(2,1)S(1)} %get-tuple-element.104.refs_1_), channel_id=1, source_target_pairs={{0,2},{1,17},{2,0},{3,19},{16,18},{17,1},{18,16},{19,3},{4,6},{5,2... | collective-permute-start | bytes 1179656 | tf_op jit(solution)/shard_map/ppermute | solution.py:87
  5.1 10.9 %collective-permute-start.24 = (bf16[384,512]{1,0:T(8,128)(2,1)S(1)}, bf16[384,512]{1,0:T(8,128)(2,1)S(1)}, u32[]{:S(2)}, u32[]{:S(2)}) collective-permute-start(bf16[384,512]{1,0:T(8,128)(2,1)S(1)} %get-tuple-element.104.refs_1_), channel_id=1, source_target_pairs={{0,16},{1,3},{2,18},{3,1},{16,0},{17,19},{18,2},{19,17},{4,20},{5,... | collective-permute-start | bytes 1179656 | tf_op jit(solution)/shard_map/ppermute | solution.py:87
  6.3 4.8 %collective-permute-start.26 = (bf16[512,128]{1,0:T(8,128)(2,1)S(1)}, bf16[512,128]{1,0:T(8,128)(2,1)S(1)}, u32[]{:S(2)}, u32[]{:S(2)}) collective-permute-start(bf16[512,128]{1,0:T(8,128)(2,1)S(1)} %get-tuple-element.95.own_ref.refs_5_), channel_id=1, source_target_pairs={{0,8},{4,12},{8,0},{12,4},{1,9},{5,13},{9,1},{13,5},{2,10},{6,14},... | collective-permute-start | bytes 393224 | tf_op jit(solution)/shard_map/ppermute | solution.py:82
  16.6 6.1 %collective-permute-start.27 = (bf16[512,128]{1,0:T(8,128)(2,1)S(1)}, bf16[512,128]{1,0:T(8,128)(2,1)S(1)}, u32[]{:S(2)}, u32[]{:S(2)}) collective-permute-start(bf16[512,128]{1,0:T(8,128)(2,1)S(1)} %get-tuple-element.100), channel_id=1, source_target_pairs={{0,4},{4,0},{8,12},{12,8},{1,5},{5,1},{9,13},{13,9},{2,6},{6,2},{1... | collective-permute-start | bytes 393224 | tf_op jit(solution)/shard_map/ppermute | solution.py:82
  18.0 8.6 %collective-permute-start.28 = (bf16[192,512]{1,0:T(8,128)(2,1)S(1)}, bf16[192,512]{1,0:T(8,128)(2,1)S(1)}, u32[]{:S(2)}, u32[]{:S(2)}) collective-permute-start(bf16[192,512]{1,0:T(8,128)(2,1)S(1)} %get-tuple-element.101), channel_id=1, source_target_pairs={{0,2},{1,17},{2,0},{3,19},{16,18},{17,1},{18,16},{19,3},{4,6},{5,2... | collective-permute-start | bytes 589832 | tf_op jit(solution)/shard_map/ppermute | solution.py:87
  18.0 7.0 %copy-start = (bf16[2,512,256]{2,1,0:T(8,128)(2,1)S(1)}, bf16[2,512,256]{2,1,0:T(8,128)(2,1)}, u32[]{:S(2)}) copy-start(bf16[2,512,256]{2,1,0:T(8,128)(2,1)} %refs_4_.5) | copy-start | bytes 1572868
  18.0 8.6 %collective-permute-start.29 = (bf16[192,512]{1,0:T(8,128)(2,1)S(1)}, bf16[192,512]{1,0:T(8,128)(2,1)S(1)}, u32[]{:S(2)}, u32[]{:S(2)}) collective-permute-start(bf16[192,512]{1,0:T(8,128)(2,1)S(1)} %get-tuple-element.110), channel_id=1, source_target_pairs={{0,16},{1,3},{2,18},{3,1},{16,0},{17,19},{18,2},{19,17},{4,20},{5,... | collective-permute-start | bytes 589832 | tf_op jit(solution)/shard_map/ppermute | solution.py:87
  22.7 4.4 %collective-permute-start.30 = (bf16[384,512]{1,0:T(8,128)(2,1)S(1)}, bf16[384,512]{1,0:T(8,128)(2,1)S(1)}, u32[]{:S(2)}, u32[]{:S(2)}) collective-permute-start(bf16[384,512]{1,0:T(8,128)(2,1)S(1)} %get-tuple-element.104.refs_1_), channel_id=1, source_target_pairs={{0,1},{1,0},{2,3},{3,2},{4,5},{5,4},{6,7},{7,6},{8,9},{9,8},{10,11... | collective-permute-start | bytes 1179656 | tf_op jit(solution)/shard_map/ppermute | solution.py:82
  24.4 2.7 %collective-permute-start.31 = (bf16[384,512]{1,0:T(8,128)(2,1)S(1)}, bf16[384,512]{1,0:T(8,128)(2,1)S(1)}, u32[]{:S(2)}, u32[]{:S(2)}) collective-permute-start(bf16[384,512]{1,0:T(8,128)(2,1)S(1)} %collective-permute-done.24.near_ref.refs_2_), channel_id=1, source_target_pairs={{0,1},{1,0},{2,3},{3,2},{4,5},{5,4},{6,7},{7,6},{8,9},{9,8},{10,11... | collective-permute-start | bytes 1179656 | tf_op jit(solution)/shard_map/ppermute | solution.py:82
  24.5 2.6 %collective-permute-start.32 = (bf16[384,512]{1,0:T(8,128)(2,1)S(1)}, bf16[384,512]{1,0:T(8,128)(2,1)S(1)}, u32[]{:S(2)}, u32[]{:S(2)}) collective-permute-start(bf16[384,512]{1,0:T(8,128)(2,1)S(1)} %collective-permute-done.25.far_ref.refs_3_), channel_id=1, source_target_pairs={{0,1},{1,0},{2,3},{3,2},{4,5},{5,4},{6,7},{7,6},{8,9},{9,8},{10,11... | collective-permute-start | bytes 1179656 | tf_op jit(solution)/shard_map/ppermute | solution.py:82
  26.6 1.6 %collective-permute-start.33 = (bf16[192,512]{1,0:T(8,128)(2,1)S(1)}, bf16[192,512]{1,0:T(8,128)(2,1)S(1)}, u32[]{:S(2)}, u32[]{:S(2)}) collective-permute-start(bf16[192,512]{1,0:T(8,128)(2,1)S(1)} %collective-permute-done.28.refs_0_), channel_id=1, source_target_pairs={{0,1},{1,0},{2,3},{3,2},{4,5},{5,4},{6,7},{7,6},{8,9},{9,8},{10,11... | collective-permute-start | bytes 589832 | tf_op jit(solution)/shard_map/ppermute | solution.py:82
  26.7 1.6 %collective-permute-start.34 = (bf16[192,512]{1,0:T(8,128)(2,1)S(1)}, bf16[192,512]{1,0:T(8,128)(2,1)S(1)}, u32[]{:S(2)}, u32[]{:S(2)}) collective-permute-start(bf16[192,512]{1,0:T(8,128)(2,1)S(1)} %collective-permute-done.29.refs_1_), channel_id=1, source_target_pairs={{0,1},{1,0},{2,3},{3,2},{4,5},{5,4},{6,7},{7,6},{8,9},{9,8},{10,11... | collective-permute-start | bytes 589832 | tf_op jit(solution)/shard_map/ppermute | solution.py:82
  30.5 4.9 %collective-permute-start.35 = (bf16[64,1024]{1,0:T(8,128)(2,1)S(1)}, bf16[64,1024]{1,0:T(8,128)(2,1)S(1)}, u32[]{:S(2)}, u32[]{:S(2)}) collective-permute-start(bf16[64,1024]{1,0:T(8,128)(2,1)S(1)} %attend.1.refs_0_), channel_id=1, source_target_pairs={{0,16},{16,0},{1,17},{17,1},{2,18},{18,2},{3,19},{19,3},{4,20},{20... | collective-permute-start | bytes 393224 | tf_op jit(solution)/shard_map/ppermute | solution.py:82
  36.3 2.6 %collective-permute-start.36 = (f32[64,2048]{1,0:T(8,128)S(1)}, f32[64,2048]{1,0:T(8,128)S(1)}, u32[]{:S(2)}, u32[]{:S(2)}) collective-permute-start(f32[64,2048]{1,0:T(8,128)S(1)} %project_sent.1), channel_id=1, source_target_pairs={{0,1},{1,0},{2,3},{3,2},{4,5},{5,4},{6,7},{7,6},{8,9},{9,8},{10,11... | collective-permute-start | bytes 1572872 | tf_op jit(solution)/shard_map/ppermute | solution.py:82
  39.0 7.6 %collective-permute-start.37 = (f32[64,1024]{1,0:T(8,128)S(1)}, f32[64,1024]{1,0:T(8,128)S(1)}, u32[]{:S(2)}, u32[]{:S(2)}) collective-permute-start(f32[64,1024]{1,0:T(8,128)S(1)} %get-tuple-element.129), channel_id=1, source_target_pairs={{0,2},{1,3},{2,0},{3,1},{4,6},{5,7},{6,4},{7,5},{8,10},{9,11},{10,... | collective-permute-start | bytes 786440 | tf_op jit(solution)/shard_map/ppermute | solution.py:82
  46.6 5.8 %collective-permute-start.1 = (bf16[64,1024]{1,0:T(8,128)(2,1)S(1)}, bf16[64,1024]{1,0:T(8,128)(2,1)}, u32[]{:S(2)}, u32[]{:S(2)}) collective-permute-start(bf16[64,1024]{1,0:T(8,128)(2,1)S(1)} %param.1), channel_id=1, source_target_pairs={{0,0},{4,4},{12,8},{8,12},{1,1},{5,5},{13,9},{9,13},{2,2},{6,6},{1... | collective-permute-start | bytes 393224 | tf_op jit(solution)/shard_map/cond/branch_1_fun/ppermute | solution.py:70
  52.5 3.5 %collective-permute-start.39 = (bf16[64,1024]{1,0:T(8,128)(2,1)}, bf16[64,1024]{1,0:T(8,128)(2,1)S(1)}, u32[]{:S(2)}, u32[]{:S(2)}) collective-permute-start(bf16[64,1024]{1,0:T(8,128)(2,1)} %get-tuple-element.132.refs_0_), channel_id=1, source_target_pairs={{0,1},{1,0},{2,3},{3,2},{4,5},{5,4},{6,7},{7,6},{8,9},{9,8},{10,11... | collective-permute-start | bytes 393224 | tf_op jit(solution)/shard_map/ppermute | solution.py:82
  54.8 5.3 %collective-permute-start.38 = (bf16[64,1024]{1,0:T(8,128)(2,1)}, bf16[64,1024]{1,0:T(8,128)(2,1)S(1)}, u32[]{:S(2)}, u32[]{:S(2)}) collective-permute-start(bf16[64,1024]{1,0:T(8,128)(2,1)} %get-tuple-element.132.refs_0_), channel_id=1, source_target_pairs={{0,2},{1,3},{2,0},{3,1},{4,6},{5,7},{6,4},{7,5},{8,10},{9,11},{10,... | collective-permute-start | bytes 393224 | tf_op jit(solution)/shard_map/ppermute | solution.py:82
  60.1 1.8 %collective-permute-start.40 = (bf16[64,1024]{1,0:T(8,128)(2,1)S(1)}, bf16[64,1024]{1,0:T(8,128)(2,1)S(1)}, u32[]{:S(2)}, u32[]{:S(2)}) collective-permute-start(bf16[64,1024]{1,0:T(8,128)(2,1)S(1)} %collective-permute-done.38.refs_0_), channel_id=1, source_target_pairs={{0,1},{1,0},{2,3},{3,2},{4,5},{5,4},{6,7},{7,6},{8,9},{9,8},{10,11... | collective-permute-start | bytes 393224 | tf_op jit(solution)/shard_map/ppermute | solution.py:82
